TPU v7x, 256 devices: a whole 4x4x8 slice. The times are simulated.
256 devices in a mesh: phase: 4 (over x), dp: 64 (over y, z, core).
Axes of the slice: x: 4, y: 4, z: 8, core: 2. Of those that a mesh axis runs over, the one named last changes fastest.
Arguments:
- tap_tokens: bfloat16 [4, 32768, 4096], P('phase', 'dp'), may hold values from -6 to 6
- project_weight: bfloat16 [4, 4096, 256], P('phase'), may hold values from -0.09375 to 0.09375
- expand_four: bfloat16 [256, 4096], replicated, may hold values from -0.375 to 0.375
- expand_two: bfloat16 [256, 1024], replicated, may hold values from -0.375 to 0.375
- shrink_weight: bfloat16 [1024, 256], replicated, may hold values from -0.1875 to 0.1875
- refine_filters: bfloat16 [4, 2, 2304, 256], P(None, None, 'dp'), may hold values from -0.125 to 0.125
- head_matrix: bfloat16 [256, 128], replicated, may hold values from -0.375 to 0.375
- head_vector: float32 [128], replicated, may hold values from -0.5 to 0.5
- tile_slot: int32 [64, 4, 8], replicated, may hold values from 0 to 1535, as said below
Outputs:
- scene_depth: float32 [1536, 256], P(('phase', 'dp'))
Inputs may be any that keep to these rules, and one draw needn't show every extreme that they name: tile_slot[d, s, j] is the slot of tile (d, s, j); it lies among the slots s * 384 to (s + 1) * 384 - 1, and every slot receives at least one tile.
All inputs are finite; a program needn't handle non-finite values.
Results may differ from a plain program's by a relative error of at most 0.015.
Values may be sent and summed in bfloat16 or wider, within the bound.
A program may use at most 128 MiB of HBM per device.

v0:
```python
import jax
import jax.numpy as jnp
from jax import lax
from jax.sharding import PartitionSpec as P

G = 32
TILES_DEV = 8
SLOT_DEV = 6


def padded_2(block, sides, width):
    for axis, dim in sides:
        count = lax.axis_size(axis)
        forward = [(i, i + 1) for i in range(count - 1)]
        backward = [(target, source) for source, target in forward]
        low = lax.ppermute(
            lax.slice_in_dim(block, block.shape[dim] - width, None, axis=dim), axis, forward
        )
        high = lax.ppermute(lax.slice_in_dim(block, 0, width, axis=dim), axis, backward)
        block = jnp.concatenate([low, block, high], axis=dim)
    return block


def from_partner(block, axis, bit):
    count = lax.axis_size(axis)
    route = []
    for low in range(count):
        high = low | 1 << bit
        if high != low and high < count:
            route += [(low, high), (high, low)]
    return lax.ppermute(block, axis, route)


def expand(feature, matrix, factor):
    height, breadth, channels = feature.shape
    flattened = jnp.dot(
        feature.reshape(height * breadth, channels), matrix, preferred_element_type=jnp.float32
    ).astype(jnp.bfloat16)
    arranged = flattened.reshape(height, breadth, factor, factor, channels).transpose(0, 2, 1, 3, 4)
    return arranged.reshape(height * factor, breadth * factor, channels)


def shrink(feature, matrix):
    height, breadth, channels = feature.shape
    blocks = feature.reshape(height // 2, 2, breadth // 2, 2, channels).transpose(0, 2, 1, 3, 4)
    blocks = blocks.reshape(height // 2 * (breadth // 2), 4 * channels)
    result = jnp.dot(blocks, matrix, preferred_element_type=jnp.float32).astype(jnp.bfloat16)
    return result.reshape(height // 2, breadth // 2, channels)


def upsample(feature):
    height, breadth, channels = feature.shape
    widened = jnp.broadcast_to(feature[:, None, :, None, :], (height, 2, breadth, 2, channels))
    return widened.reshape(2 * height, 2 * breadth, channels)


def extend(feature):
    widened = padded_2(feature, (("phase", 1),), 1)
    parity = lax.axis_index("dp") % 2
    boundary = jnp.where(parity == 0, widened[-1], widened[0])
    partner = from_partner(boundary, "dp", 0)
    zeroed = jnp.zeros_like(partner)
    upper_row = jnp.where(parity == 1, partner, zeroed)
    lower_row = jnp.where(parity == 0, partner, zeroed)
    return jnp.concatenate([upper_row[None], widened, lower_row[None]], axis=0)


def convolve(feature, matrix):
    height, breadth, channels = feature.shape
    padded = extend(feature)
    patches = jnp.concatenate(
        [
            padded[row_shift : row_shift + height, col_shift : col_shift + breadth]
            for row_shift in range(3)
            for col_shift in range(3)
        ],
        axis=-1,
    )
    patches = patches.reshape(height * breadth, 9 * channels)
    whole_matrix = lax.all_gather(matrix, "dp", axis=0, tiled=True)
    result = jnp.dot(patches, whole_matrix, preferred_element_type=jnp.float32)
    return result.reshape(height, breadth, channels)


def refine(summed, first_matrix, second_matrix):
    inner_map = convolve(jax.nn.relu(summed).astype(jnp.bfloat16), first_matrix)
    branch = convolve(jax.nn.relu(inner_map).astype(jnp.bfloat16), second_matrix)
    return (summed + branch).astype(jnp.bfloat16)


def per_device(
    tap_tokens,
    project_weight,
    expand_four,
    expand_two,
    shrink_weight,
    refine_filters,
    head_matrix,
    head_vector,
    tile_slot,
):
    token_rows = tap_tokens.shape[1] // G
    channels = project_weight.shape[2]
    projected = jnp.dot(
        tap_tokens[0], project_weight[0], preferred_element_type=jnp.float32
    ).astype(jnp.bfloat16)
    projected = projected.reshape(1, token_rows, G, channels)
    quarters = lax.all_to_all(projected, "phase", split_axis=2, concat_axis=0, tiled=True)
    inputs = [
        expand(quarters[0], expand_four, 4),
        expand(quarters[1], expand_two, 2),
        quarters[2],
        shrink(quarters[3], shrink_weight),
    ]
    joined_map = refine(inputs[3].astype(jnp.float32), refine_filters[3, 0], refine_filters[3, 1])
    for level_id in (2, 1, 0):
        summed = inputs[level_id].astype(jnp.float32) + upsample(joined_map).astype(jnp.float32)
        joined_map = refine(summed, refine_filters[level_id, 0], refine_filters[level_id, 1])
    hidden = jax.nn.relu(
        jnp.dot(joined_map.reshape(-1, channels), head_matrix, preferred_element_type=jnp.float32)
    )
    depth_map = jnp.dot(hidden, head_vector, precision=lax.Precision.HIGHEST)
    depth_tiles = depth_map.reshape(TILES_DEV, -1)
    phase_id = lax.axis_index("phase")
    dp_id = lax.axis_index("dp")
    dp_count = lax.axis_size("dp")
    owned_slots = (phase_id * dp_count + dp_id) * SLOT_DEV + jnp.arange(SLOT_DEV, dtype=jnp.int32)
    portion = lax.all_gather(depth_tiles[None], "dp", axis=0, tiled=True)
    targets = lax.dynamic_index_in_dim(tile_slot, phase_id, 1, keepdims=False).reshape(-1)
    matches = (owned_slots[:, None] == targets[None, :]).astype(jnp.float32)
    return jnp.dot(matches, portion.reshape(-1, portion.shape[-1]), precision=lax.Precision.HIGHEST)


def solution(mesh):
    in_specs = (
        P("phase", "dp", None),
        P("phase", None, None),
        P(),
        P(),
        P(),
        P(None, None, "dp", None),
        P(),
        P(),
        P(),
    )
    out_specs = P(("phase", "dp"), None)
    return jax.shard_map(
        per_device, mesh=mesh, in_specs=in_specs, out_specs=out_specs, check_vma=False
    )
```

profile of v0, /device:TPU:1, one launch (start us, length us, event | category | flops | bytes accessed | tf_op | source)
XLA Modules:
  0.0 702.9 jit_solution(16663639851343577037)
XLA Ops:
  6.5 2.0 slice_bitcast_fusion.5
  9.4 4.2 fusion.6
  13.7 10.2 %all_to_all.15 = bf16[1,16,32,256]{3,1,0,2:T(8,128)(2,1)S(1)} all-to-all(bf16[1,16,32,256]{3,1,0,2:T(8,128)(2,1)S(1)} %copy.178), channel_id=1, replica_groups=mesh['phase'=4,'dp'=64] {'phase'}, dimensions={2} | all-to-all | bytes 524288 | tf_op jit(solution)/shard_map/all_to_all | solution.py:108
  25.7 4.0 collective-permute-start
  30.4 3.3 collective-permute-start.2
  34.8 57.1 %all-gather.17.cloned.1.call-done = bf16[1,1,2304,256]{3,1,0,2:T(2,128)(2,1)} async-done(((bf16[1,1,36,256]{3,1,0,2:T(2,128)(2,1)}), bf16[1,1,2304,256]{3,1,0,2:T(2,128)(2,1)}) %all-gather.17.cloned.1.call-update) | async-done | bytes 1179664 | tf_op jit(solution)/shard_map/all_gather | solution.py:80
  95.2 4.0 collective-permute-start.3
  102.4 67.4 %all-gather.19.cloned.1.call-done = bf16[1,1,2304,256]{3,1,0,2:T(2,128)(2,1)} async-done(((bf16[1,1,36,256]{3,1,0,2:T(2,128)(2,1)}), bf16[1,1,2304,256]{3,1,0,2:T(2,128)(2,1)}) %all-gather.19.cloned.1.call-update) | async-done | bytes 1179664 | tf_op jit(solution)/shard_map/all_gather | solution.py:80
  173.3 4.0 collective-permute-start.6
  186.5 61.1 %all-gather.21.cloned.1.call-done = bf16[1,1,2304,256]{3,1,0,2:T(2,128)(2,1)} async-done(((bf16[1,1,36,256]{3,1,0,2:T(2,128)(2,1)}), bf16[1,1,2304,256]{3,1,0,2:T(2,128)(2,1)}) %all-gather.21.cloned.1.call-update) | async-done | bytes 1179664 | tf_op jit(solution)/shard_map/all_gather | solution.py:80
  247.7 2.2 fusion.43
  251.2 4.0 collective-permute-start.9
  258.8 66.7 %all-gather.23.cloned.1.call-done = bf16[1,1,2304,256]{3,1,0,2:T(2,128)(2,1)} async-done(((bf16[1,1,36,256]{3,1,0,2:T(2,128)(2,1)}), bf16[1,1,2304,256]{3,1,0,2:T(2,128)(2,1)}) %all-gather.23.cloned.1.call-update) | async-done | bytes 1179664 | tf_op jit(solution)/shard_map/all_gather | solution.py:80
  325.4 2.0 fusion.40
  329.6 4.0 collective-permute-start.12
  344.5 58.6 %all-gather.25.cloned.1.call-done = bf16[1,1,2304,256]{3,1,0,2:T(2,128)(2,1)} async-done(((bf16[1,1,36,256]{3,1,0,2:T(2,128)(2,1)}), bf16[1,1,2304,256]{3,1,0,2:T(2,128)(2,1)}) %all-gather.25.cloned.1.call-update) | async-done | bytes 1179664 | tf_op jit(solution)/shard_map/all_gather | solution.py:80
  403.2 3.2 fusion.3
  407.7 4.0 collective-permute-start.15
  414.6 2.3 copy.181
  416.9 2.0 reshape.106
  426.6 54.3 %all-gather.27.cloned.1.call-done = bf16[1,1,2304,256]{3,1,0,2:T(2,128)(2,1)} async-done(((bf16[1,1,36,256]{3,1,0,2:T(2,128)(2,1)}), bf16[1,1,2304,256]{3,1,0,2:T(2,128)(2,1)}) %all-gather.27.cloned.1.call-update) | async-done | bytes 1179664 | tf_op jit(solution)/shard_map/all_gather | solution.py:80
  480.9 3.2 fusion.5
  484.1 2.3 broadcast_in_dim.81
  486.4 3.7 convert_element_type.127
  490.1 3.4 maximum_convert_fusion.1
  494.9 4.0 collective-permute-start.18
  517.7 41.1 %all-gather.29.cloned.1.call-done = bf16[1,1,2304,256]{3,1,0,2:T(2,128)(2,1)} async-done(((bf16[1,1,36,256]{3,1,0,2:T(2,128)(2,1)}), bf16[1,1,2304,256]{3,1,0,2:T(2,128)(2,1)}) %all-gather.29.cloned.1.call-update) | async-done | bytes 1179664 | tf_op jit(solution)/shard_map/all_gather | solution.py:80
  558.8 7.0 maximum_convert_fusion
  567.2 4.0 collective-permute-start.21
  590.0 46.7 %all-gather.31.cloned.1.call-done = bf16[1,1,2304,256]{3,1,0,2:T(2,128)(2,1)} async-done(((bf16[1,1,36,256]{3,1,0,2:T(2,128)(2,1)}), bf16[1,1,2304,256]{3,1,0,2:T(2,128)(2,1)}) %all-gather.31.cloned.1.call-update) | async-done | bytes 1179664 | tf_op jit(solution)/shard_map/all_gather | solution.py:80
  636.7 7.8 %add_convert_fusion = bf16[64,32,256]{2,1,0:T(8,128)(2,1)S(1)} fusion(f32[64,32,256]{2,1,0:T(8,128)} %get-tuple-element.6, bf16[64,32,2304]{2,1,0:T(8,128)(2,1)} %slice_dynamic-update-slice_fusion, bf16[1,1,2304,256]{3,1,0,2:T(2,128)(2,1)} %all-gather.31.cloned.1.call-done), kind=kOutput, calls=%fused_computation.6 | convolution fusion | flops 2416967680 | bytes 13762560 | tf_op jit(solution)/shard_map/dot_general | solution.py:81
  645.9 48.8 %all_gather.35 = f32[64,8,256]{2,1,0:T(8,128)S(1)} all-gather(f32[1,8,256]{2,1,0:T(8,128)S(1)} %broadcast_in_dim_reshape.4), channel_id=1, replica_groups=mesh['phase'=4,'dp'=64] {'dp'}, dimensions={0}, use_global_device_ids=true | all-gather | bytes 532480 | tf_op jit(solution)/shard_map/all_gather | solution.py:128
  (213 shorter events, 95.7 us)
Async XLA Ops:
  6.5 85.4 %all-gather.17.cloned.1.call-start = ((), (), s32[]{:S(2)}) async-start(), calls=%async_computation.1 | async-start | bytes 2396160 | tf_op jit(solution)/shard_map/all_gather | solution.py:80
  8.6 161.2 %all-gather.19.cloned.1.call-start = ((), (), s32[]{:S(2)}) async-start(), calls=%async_computation.2 | async-start | bytes 2396160 | tf_op jit(solution)/shard_map/all_gather | solution.py:80
  9.3 238.4 %all-gather.21.cloned.1.call-start = ((), (), s32[]{:S(2)}) async-start(), calls=%async_computation.3 | async-start | bytes 2396160 | tf_op jit(solution)/shard_map/all_gather | solution.py:80
  24.4 5.3 collective-permute-start.1
  25.7 4.7 collective-permute-start
  30.4 4.1 collective-permute-start.2
  33.8 291.6 %all-gather.23.cloned.1.call-start = ((), (), s32[]{:S(2)}) async-start(), calls=%async_computation.4 | async-start | bytes 2396160 | tf_op jit(solution)/shard_map/all_gather | solution.py:80
  93.9 5.3 collective-permute-start.4
  95.2 4.7 collective-permute-start.3
  100.0 2.3 collective-permute-start.5
  101.4 301.7 %all-gather.25.cloned.1.call-start = ((), (), s32[]{:S(2)}) async-start(), calls=%async_computation.5 | async-start | bytes 2396160 | tf_op jit(solution)/shard_map/all_gather | solution.py:80
  172.0 5.3 collective-permute-start.7
  173.3 4.8 collective-permute-start.6
  178.2 2.3 collective-permute-start.8
  179.7 301.3 %all-gather.27.cloned.1.call-start = ((), (), s32[]{:S(2)}) async-start(), calls=%async_computation.6 | async-start | bytes 2396160 | tf_op jit(solution)/shard_map/all_gather | solution.py:80
  249.9 5.4 collective-permute-start.10
  251.2 4.8 collective-permute-start.9
  255.2 303.6 %all-gather.29.cloned.1.call-start = ((), (), s32[]{:S(2)}) async-start(), calls=%async_computation.7 | async-start | bytes 2396160 | tf_op jit(solution)/shard_map/all_gather | solution.py:80
  256.1 2.3 collective-permute-start.11
  328.3 5.3 collective-permute-start.13
  329.6 5.0 collective-permute-start.12
  334.6 2.3 collective-permute-start.14
  336.1 300.6 %all-gather.31.cloned.1.call-start = ((), (), s32[]{:S(2)}) async-start(), calls=%async_computation.8 | async-start | bytes 2396160 | tf_op jit(solution)/shard_map/all_gather | solution.py:80
  406.4 6.6 collective-permute-start.16
  407.7 5.3 collective-permute-start.15
  413.0 5.9 collective-permute-start.17
  493.6 5.3 collective-permute-start.19
  494.9 5.3 collective-permute-start.18
  500.2 2.5 collective-permute-start.20
  565.9 6.0 collective-permute-start.22
  567.2 5.3 collective-permute-start.21
  572.5 2.6 collective-permute-start.23
  (9 other events, 956.9 us)
Sparse Core Ops, SparseCore 0:
  10.1 81.8 all-gather.16
  94.6 75.1 all-gather.18
  172.5 75.1 all-gather.20
  250.2 75.1 all-gather.22
  328.0 75.1 all-gather.24
  405.7 75.1 all-gather.26
  483.6 75.1 all-gather.28
  561.5 75.1 all-gather.30
where the time goes:
time: 712 us; the launch traced here: 703 us
  waiting for transfers between devices  465 us (65%)
  blocking collectives  59 us (8%)
  starting transfers between devices  56.4 us (8%)
  local copies, waits for them, and re-layouts  50 us (7%)
  matrix products  37.3 us (5%)
  other arithmetic  20.4 us (3%)
  between operations  14.9 us (2%)
    all_gather x8, waiting for transfers between devices, convolve(): whole_matrix = lax.all_gather(matrix, 'dp', axis=0, tiled=True)  453 us
    all_gather x1, blocking collectives, per_device(): portion = lax.all_gather(depth_tiles[None], 'dp', axis=0, tiled=True)  48.8 us
    ppermute x8, starting transfers between devices, padded_2(): lax.ppermute(lax.slice_in_dim(block, block.shape[dim] - width, None, axis...  31.9 us
    unnamed x67, local copies, waits for them, and re-layouts  31.7 us
    dot_general x8, matrix products, convolve(): result = jnp.dot(patches, whole_matrix, preferred_element_type=jnp.float32)  29.1 us
  transfers between devices with their start and end apart: 32, of which 22 were waited for; matrix products, arithmetic and copies ran while one was open for 14% of the time, Pallas kernels for 0%

commit v1 on v0

v1 whole, which is shorter than its diff:
```python
import jax
import jax.numpy as jnp
from jax import lax
from jax.experimental import pallas as pl
from jax.experimental.pallas import tpu as pltpu
from jax.sharding import PartitionSpec as P

MESH = pl.DeviceIdType.MESH
BF = jnp.bfloat16
F32 = jnp.float32
CH = 256
SLOT_DEV = 6
BLOCK = 288

OWN = (8, 8, 8, 2)
HALO = (1, 2, 4, 2)
SENT = (10, 12, 16, 6)
LEN = (12, 16, 24, 10)


def coords():
    phase, dp = lax.axis_index("phase"), lax.axis_index("dp")
    return phase, dp // 16, (dp // 2) % 8, dp % 2


def did(x, y, z, c):
    return (x, (y * 8 + z) * 2 + c)


def kernel(
    tap_hbm, weight_hbm, four_hbm, two_hbm, shrink_hbm, filter_hbm, head_ref, vector_ref, target_ref,
    out_ref,
    filt, own, zbuf, rel, tap, weight, four, two, shrink, proj, gathered, sent,
    rb0, rb1, rb2, rb3, lift, tok0, tok1, spread,
    s0, s1, s2, s3, i0, i1, i2, i3, j0, j1, j2, j3, b0, b1, b2, b3, tiles,
    own_sem, tap_sem, load_sem, zs, zr, ys, yr, xs, xr, cs, cr, ts, tr, fs, fr, us, ur, vs, vr, ws, wr,
):
    x, y, z, c = coords()
    e = x % 2
    ct = z // 4
    slot = (z % 4) * 2 + c
    received = (rb0, rb1, rb2, rb3)

    own_load = pltpu.make_async_copy(filter_hbm, own, own_sem)
    own_load.start()
    weight_load = pltpu.make_async_copy(weight_hbm.at[0], weight, load_sem.at[0])
    weight_load.start()
    tap_loads = [
        pltpu.make_async_copy(tap_hbm.at[0, pl.ds(128 * k, 128)], tap.at[pl.ds(128 * k, 128)], tap_sem.at[k])
        for k in range(4)
    ]
    for load in tap_loads:
        load.start()
    shrink_load = pltpu.make_async_copy(shrink_hbm, shrink, load_sem.at[1])
    four_load = pltpu.make_async_copy(four_hbm, four, load_sem.at[2])
    two_load = pltpu.make_async_copy(two_hbm, two, load_sem.at[3])
    for load in (shrink_load, four_load, two_load):
        load.start()

    for k in range(4):
        received[k][...] = jnp.zeros_like(received[k])

    barrier = pltpu.get_barrier_semaphore()
    for dz in range(8):
        for dc in range(2):
            if dz or dc:
                pl.semaphore_signal(barrier, inc=1, device_id=did(x, y, (z + dz) % 8, (c + dc) % 2), device_id_type=MESH)
    for step in range(1, 4):
        pl.semaphore_signal(barrier, inc=1, device_id=did(x, (y + step) % 4, z, c), device_id_type=MESH)
        pl.semaphore_signal(barrier, inc=1, device_id=did((x + step) % 4, y, z, c), device_id_type=MESH)
    own_load.wait()
    pl.semaphore_wait(barrier, 21)

    def zcopy(L, dz):
        return pltpu.make_async_remote_copy(
            src_ref=own.at[L, e], dst_ref=zbuf.at[L, slot], send_sem=zs.at[L, dz], recv_sem=zr.at[L, slot],
            device_id=did(x, y, (z + dz) % 8, ct), device_id_type=MESH)

    def zsend(L):
        for dz in (4, 3, 5, 2, 6, 1, 7):
            zcopy(L, dz).start()

        @pl.when(ct == c)
        def _():
            pltpu.make_async_copy(own.at[L, e], zbuf.at[L, slot], zr.at[L, slot]).start()

        @pl.when(ct != c)
        def _():
            zcopy(L, 0).start()

    def block(dy, cc, count=BLOCK, start=0):
        return pl.ds(pl.multiple_of((((y + 4 - dy) % 4) * 2 + cc) * BLOCK + start, 16), count)

    def ycopy(L, dy, back):
        ref = filt.at[2 * L + e, block(back, c)]
        return pltpu.make_async_remote_copy(
            src_ref=ref, dst_ref=ref, send_sem=ys.at[L, dy], recv_sem=yr.at[L, dy],
            device_id=did(x, (y + dy) % 4, z, c), device_id_type=MESH)

    def xcopy(L, dy, h, f):
        ref = filt.at[2 * L + f, block(dy, c, 144, 144 * h)]
        return pltpu.make_async_remote_copy(
            src_ref=ref, dst_ref=ref, send_sem=xs.at[L, dy, h], recv_sem=xr.at[L, dy, h],
            device_id=did((x + 1 + 2 * h) % 4, y, z, c), device_id_type=MESH)

    def ccopy(L, dy, f, cc, count, start, k):
        ref = filt.at[2 * L + f, block(dy, cc, count, start)]
        return pltpu.make_async_remote_copy(
            src_ref=ref, dst_ref=ref, send_sem=cs.at[L, k], recv_sem=cr.at[L, k],
            device_id=did(x, y, z, 1 - c), device_id_type=MESH)

    def forward(L, dy):
        xcopy(L, dy, 0, e).start()
        xcopy(L, dy, 1, e).start()
        ccopy(L, dy, e, c, BLOCK, 0, dy).start()

    def zy(L):
        for s in range(8):
            pltpu.make_async_copy(own.at[L, e], zbuf.at[L, s], zr.at[L, s]).wait()
        for s in range(8):
            rel[pl.ds(36 * s, 36)] = zbuf[L, s].astype(F32)
        filt[2 * L + e, block(0, c)] = rel[...].astype(BF)
        for dy in (2, 1, 3):
            ycopy(L, dy, 0).start()
        forward(L, 0)

    def yx(L):
        for dy in (1, 3, 2):
            ycopy(L, dy, dy).wait_recv()
            forward(L, dy)

    def xc(L):
        for dy in (0, 1, 3, 2):
            for h in range(2):
                xcopy(L, dy, h, 1 - e).wait_recv()
                ccopy(L, dy, 1 - e, c, 144, 144 * h, 4 + dy * 2 + h).start()

    def fin(L):
        for dy in range(4):
            ccopy(L, dy, e, 1 - c, BLOCK, 0, dy).wait_recv()
            for h in range(2):
                ccopy(L, dy, 1 - e, 1 - c, 144, 144 * h, 4 + dy * 2 + h).wait_recv()

    def sent_filters(L):
        for dz in range(1, 8):
            zcopy(L, dz).wait_send()

        @pl.when(ct != c)
        def _():
            zcopy(L, 0).wait_send()

        for dy in range(1, 4):
            ycopy(L, dy, 0).wait_send()
        for dy in range(4):
            ccopy(L, dy, e, c, BLOCK, 0, dy).wait_send()
            for h in range(2):
                xcopy(L, dy, h, e).wait_send()
                ccopy(L, dy, 1 - e, c, 144, 144 * h, 4 + dy * 2 + h).wait_send()

    for L in (3, 2, 1, 0):
        zsend(L)

    weight_load.wait()
    for k in range(4):
        tap_loads[k].wait()
        part = jnp.dot(tap[pl.ds(128 * k, 128)], weight[...], preferred_element_type=F32)
        for n in range(2):
            proj[n, pl.ds(128 * k, 128)] = part[:, 128 * n:128 * n + 128]
    shrink_load.wait()

    @pl.when(x == 3)
    def _():
        for j in range(16):
            for a in range(2):
                for b in range(2):
                    for n in range(2):
                        gathered[pl.ds(8 * j, 8), pl.ds((2 * a + b) * CH + 128 * n, 128)] = (
                            proj[n, pl.ds(a * 32 + 2 * j + b, 8, 64)])
        mixed = jnp.dot(gathered[...].astype(BF), shrink[...], preferred_element_type=F32)
        sent[pl.ds(0, 8)] = mixed.astype(BF).reshape(8, 16, CH)

    @pl.when(x != 3)
    def _():
        for j in range(32):
            for n in range(2):
                sent[j, :, pl.ds(128 * n, 128)] = proj[n, pl.ds(j, 16, 32)].astype(BF)

    def offset(k, s):
        return HALO[k] * (2 - (s + 1) // 2)

    def window(k, cc, s):
        return received[k].at[cc, pl.ds(offset(k, s), SENT[k])]

    def start_of(k, s):
        return OWN[k] * s - 2 * HALO[k] + offset(k, s)

    def tap_copy(k, s, n):
        return pltpu.make_async_remote_copy(
            src_ref=sent.at[pl.ds(start_of(k, s), SENT[k])], dst_ref=window(k, c, s), send_sem=ts.at[n], recv_sem=tr.at[k],
            device_id=did(s, y, z, c), device_id_type=MESH)

    for k in range(4):
        @pl.when(x == k)
        def _():
            for n in (2, 1, 3):
                tap_copy(k, (k + n) % 4, n).start()
            pltpu.make_async_copy(sent.at[pl.ds(start_of(k, k), SENT[k])], window(k, c, k), tr.at[k]).start()

    def halves(k, cc):
        ref = window(k, cc, x)
        return pltpu.make_async_remote_copy(
            src_ref=ref, dst_ref=ref, send_sem=fs.at[k], recv_sem=fr.at[k], device_id=did(x, y, z, 1 - c), device_id_type=MESH)

    for k in (3, 2, 1, 0):
        pltpu.make_async_copy(sent.at[pl.ds(0, SENT[k])], window(k, c, x), tr.at[k]).wait()
        halves(k, c).start()
    zy(3)
    zy(2)

    upper = c == 0
    lift[...] = jnp.zeros_like(lift)

    def rows_of(k, col, height, halo, count):
        lift[pl.ds(16, 16)] = received[k][0, col].astype(F32)
        lift[pl.ds(32, 16)] = received[k][1, col].astype(F32)
        return jnp.where(upper, lift[pl.ds(16 - halo, count)], lift[pl.ds(32 - halo, count)])

    def put(s, col, rows, value):
        for n in range(2):
            s[n, col, pl.ds(0, rows)] = value[:, 128 * n:128 * n + 128]

    halves(3, 1 - c).wait_recv()

    def load_3(pair, _):
        low = rb3[0, 2 + pair].astype(F32)
        high = rb3[1, 2 + pair].astype(F32)
        blank = jnp.zeros((8, CH), F32)
        for n in range(2):
            lift[pl.ds(8, 8)] = blank
            lift[pl.ds(16, 8)] = low[8 * n:8 * n + 8]
            lift[pl.ds(24, 8)] = high[8 * n:8 * n + 8]
            lift[pl.ds(32, 8)] = blank
            put(s3, 2 * pair + n, 16, jnp.where(upper, lift[pl.ds(12, 16)], lift[pl.ds(20, 16)]))
        return _

    lax.fori_loop(0, 6, load_3, 0)
    halves(2, 1 - c).wait_recv()
    lift[...] = jnp.zeros_like(lift)

    def load_2(col, _):
        put(s2, col, 24, rows_of(2, 4 + col, 16, 4, 24))
        return _

    lax.fori_loop(0, 16, load_2, 0)
    halves(1, 1 - c).wait_recv()

    def load_1(col, _):
        tok1[col] = rows_of(1, 2 + col, 16, 2, 32).astype(BF)
        return _

    lax.fori_loop(0, 12, load_1, 0)
    halves(0, 1 - c).wait_recv()

    def load_0(col, _):
        tok0[col] = rows_of(0, 1 + col, 16, 1, 32).astype(BF)
        return _

    lax.fori_loop(0, 10, load_0, 0)

    two_load.wait()
    for a in range(2):
        for b in range(2):
            part = jnp.dot(tok1[...].reshape(384, CH), two[:, pl.ds((2 * a + b) * CH, CH)], preferred_element_type=F32)
            spread[...] = part.astype(BF).astype(F32).reshape(12, 32, CH)

            def place_1(col, _, a=a, b=b):
                for n in range(2):
                    s1[n, 2 * col + b, pl.ds(a, 20, 2)] = spread[col, pl.ds(0, 20), pl.ds(128 * n, 128)]
                return _

            lax.fori_loop(0, 12, place_1, 0)
    yx(3)
    zy(1)
    four_load.wait()
    for a in range(4):
        for b in range(4):
            part = jnp.dot(tok0[...].reshape(320, CH), four[:, pl.ds((4 * a + b) * CH, CH)], preferred_element_type=F32)
            spread[pl.ds(0, 10)] = part.astype(BF).astype(F32).reshape(10, 32, CH)
            first_row, first_col = int(a < 2), int(b < 2)

            def place_0(col, _, a=a, b=b, first_row=first_row, first_col=first_col):
                for n in range(2):
                    s0[n, 4 * (col + first_col) + b - 2, pl.ds(4 * first_row + a - 2, 17, 4)] = (
                        spread[col + first_col, pl.ds(first_row, 17), pl.ds(128 * n, 128)])
                return _

            lax.fori_loop(0, 9, place_0, 0)

    def inside(col, out_halo, own_cols, own_rows, rows):
        row = lax.broadcasted_iota(jnp.int32, (1, rows, 1), 1) + (own_rows * c - out_halo)
        cols = lax.broadcasted_iota(jnp.int32, (col[1], 1, 1), 0) + (own_cols * x - out_halo + col[0])
        return (row >= 0) & (row < 2 * own_rows) & (cols >= 0) & (cols < 4 * own_cols)

    def build(source, target, col_start, row_start, cols, rows):
        def step(col, _):
            for p in range(3):
                if len(source.shape) == 4:
                    piece = jnp.concatenate([source[n, col + col_start, pl.ds(row_start + p, rows)] for n in range(2)], axis=-1)
                else:
                    piece = source[col + col_start, pl.ds(row_start + p, rows)]
                target[p, col, pl.ds(0, rows)] = jnp.maximum(piece, 0.0).astype(BF)
            return _

        lax.fori_loop(0, cols, step, 0)

    def conv(source, f, cols, rows, chunk, emit):
        def step(at, _):
            start = at * chunk
            patches = jnp.concatenate(
                [source[p, pl.ds(start + q, chunk), pl.ds(0, rows)].reshape(chunk * rows, CH) for p in range(3) for q in range(3)],
                axis=1)
            result = jnp.dot(patches, filt[f], preferred_element_type=F32)
            emit(start, result.reshape(chunk, rows, CH))
            return _

        lax.fori_loop(0, cols // chunk, step, 0)

    def level(k, s, inner, joined, patch, own_cols, own_rows, first, second):
        halo1, cols1, rows1, chunk1, col0, row0 = first
        halo2, cols2, rows2, chunk2, at = second
        build(s, patch, col0, row0, cols1 + 2, rows1)

        def emit_1(start, result):
            keep = inside((start, chunk1), halo1, own_cols, own_rows, rows1)
            inner[pl.ds(start, chunk1), pl.ds(0, rows1)] = jnp.where(keep, result, 0.0)

        conv(patch, 2 * k, cols1, rows1, chunk1, emit_1)
        build(inner, patch, 0, 0, cols2 + 2, rows2)

        def emit_2(start, result):
            keep = inside((start, chunk2), halo2, own_cols, own_rows, rows2)
            before = jnp.concatenate([s[n, pl.ds(start + at, chunk2), pl.ds(at, rows2)] for n in range(2)], axis=-1)
            total = (before + result).astype(BF).astype(F32)
            joined[pl.ds(start, chunk2)] = jnp.where(keep, total, 0.0)

        conv(patch, 2 * k + 1, cols2, rows2, chunk2, emit_2)

    def rise(joined, s, cols, rows):
        def step(col, _):
            for n in range(2):
                piece = joined[col, pl.ds(0, rows), pl.ds(128 * n, 128)]
                for a in range(2):
                    for b in range(2):
                        at = (n, 2 * col + b, pl.ds(a, rows, 2))
                        s[at] = s[at] + piece
            return _

        lax.fori_loop(0, cols, step, 0)

    xc(3)
    yx(2)
    zy(0)
    fin(3)
    level(3, s3, i3, j3, b3, 4, 8, (3, 10, 16, 10, 0, 0), (2, 8, 16, 8, 2))
    rise(j3, s2, 8, 12)
    xc(2)
    yx(1)
    fin(2)
    level(2, s2, i2, j2, b2, 8, 16, (3, 14, 32, 14, 0, 0), (2, 12, 32, 12, 2))
    rise(j2, s1, 12, 20)
    xc(1)
    yx(0)
    fin(1)
    level(1, s1, i1, j1, b1, 16, 32, (2, 20, 48, 10, 1, 1), (1, 18, 48, 9, 3))
    rise(j1, s0, 18, 34)
    xc(0)
    fin(0)
    level(0, s0, i0, j0, b0, 32, 64, (1, 34, 80, 2, 0, 0), (0, 32, 64, 4, 2))

    for t in range(8):
        feature = j0[:, pl.ds(8 * t, 8)].reshape(256, CH).astype(BF)
        hidden = jnp.maximum(jnp.dot(feature, head_ref[...], preferred_element_type=F32), 0.0)
        depth = lax.dot_general(
            jnp.broadcast_to(vector_ref[...], (8, 128)), hidden, (((1,), (1,)), ((), ())),
            precision=lax.Precision.HIGHEST, preferred_element_type=F32)
        for n in range(2):
            rel[pl.ds(8 * n + t, 1), pl.ds(0, 128)] = depth[0:1, 128 * n:128 * n + 128]
    tiles[c, y, z] = rel[pl.ds(0, 16), pl.ds(0, 128)].astype(BF)

    def ucopy(dz, back):
        ref = tiles.at[c, y, (z + 8 - back) % 8]
        return pltpu.make_async_remote_copy(
            src_ref=ref, dst_ref=ref, send_sem=us.at[dz], recv_sem=ur.at[dz], device_id=did(x, y, (z + dz) % 8, c), device_id_type=MESH)

    def vcopy(dy, back):
        ref = tiles.at[c, (y + 4 - back) % 4]
        return pltpu.make_async_remote_copy(
            src_ref=ref, dst_ref=ref, send_sem=vs.at[dy], recv_sem=vr.at[dy], device_id=did(x, (y + dy) % 4, z, c), device_id_type=MESH)

    def wcopy(dy, cc):
        ref = tiles.at[cc, (y + 4 - dy) % 4]
        return pltpu.make_async_remote_copy(
            src_ref=ref, dst_ref=ref, send_sem=ws.at[dy], recv_sem=wr.at[dy], device_id=did(x, y, z, 1 - c), device_id_type=MESH)

    for dz in (4, 3, 5, 2, 6, 1, 7):
        ucopy(dz, 0).start()
    for L in (3, 2, 1, 0):
        sent_filters(L)
    for k in range(4):
        @pl.when(x == k)
        def _():
            for n in range(1, 4):
                tap_copy(k, (k + n) % 4, n).wait_send()
        halves(k, c).wait_send()
    slots = (x * 64 + (y * 8 + z) * 2 + c) * SLOT_DEV
    row = lax.broadcasted_iota(jnp.int32, (16, 1024), 0)
    wanted = (slots + row % 8) * 2 + row // 8
    match = jnp.where(target_ref[...] == wanted, 1.0, 0.0).astype(BF)
    for dz in range(1, 8):
        ucopy(dz, dz).wait_recv()
    for dy in (2, 1, 3):
        vcopy(dy, 0).start()
    wcopy(0, c).start()
    for dy in (1, 3, 2):
        vcopy(dy, dy).wait_recv()
        wcopy(dy, c).start()
    for dy in range(4):
        wcopy(dy, 1 - c).wait_recv()
    out_ref[...] = jnp.dot(match, tiles[...].reshape(1024, 128), preferred_element_type=F32)
    for dz in range(1, 8):
        ucopy(dz, 0).wait_send()
    for dy in range(1, 4):
        vcopy(dy, 0).wait_send()
    for dy in range(4):
        wcopy(dy, c).wait_send()


def per_device(
    tap_tokens, project_weight, expand_four, expand_two, shrink_weight, refine_filters, head_matrix, head_vector, tile_slot
):
    phase = lax.axis_index("phase")
    mine = lax.dynamic_index_in_dim(tile_slot, phase, 1, keepdims=False).reshape(4, 8, 2, 1, 8).transpose(2, 0, 1, 3, 4)
    target = (mine * 2 + jnp.arange(2, dtype=jnp.int32).reshape(1, 1, 1, 2, 1)).reshape(1, 1024)
    vmem, dma = pltpu.VMEM, pltpu.SemaphoreType.DMA
    anywhere = pl.BlockSpec(memory_space=pl.ANY)
    inside = pl.BlockSpec(memory_space=pltpu.VMEM)
    result = pl.pallas_call(
        kernel,
        out_shape=jax.ShapeDtypeStruct((16, 128), F32),
        in_specs=[anywhere] * 6 + [inside] * 3,
        out_specs=inside,
        scratch_shapes=[
            vmem((8, 2304, CH), BF), vmem((4, 2, 36, CH), BF), vmem((4, 8, 36, CH), BF), vmem((BLOCK, CH), F32),
            vmem((512, 4096), BF), vmem((4096, CH), BF), vmem((CH, 4096), BF), vmem((CH, 1024), BF), vmem((1024, CH), BF),
            vmem((2, 512, 128), F32), vmem((128, 1024), F32), vmem((32, 16, CH), BF),
            vmem((2, LEN[0], 16, CH), BF), vmem((2, LEN[1], 16, CH), BF), vmem((2, LEN[2], 16, CH), BF), vmem((2, LEN[3], 16, CH), BF),
            vmem((64, CH), F32), vmem((10, 32, CH), BF), vmem((12, 32, CH), BF), vmem((12, 32, CH), F32),
            vmem((2, 36, 88, 128), F32), vmem((2, 24, 56, 128), F32), vmem((2, 16, 40, 128), F32), vmem((2, 12, 24, 128), F32),
            vmem((34, 88, CH), F32), vmem((20, 56, CH), F32), vmem((14, 40, CH), F32), vmem((10, 24, CH), F32),
            vmem((32, 64, CH), F32), vmem((18, 48, CH), F32), vmem((12, 32, CH), F32), vmem((8, 16, CH), F32),
            vmem((3, 36, 80, CH), BF), vmem((3, 22, 48, CH), BF), vmem((3, 16, 32, CH), BF), vmem((3, 12, 16, CH), BF),
            vmem((2, 4, 8, 16, 128), BF),
            dma, dma((4,)), dma((4,)), dma((4, 8)), dma((4, 8)), dma((4, 4)), dma((4, 4)), dma((4, 4, 2)), dma((4, 4, 2)),
            dma((4, 12)), dma((4, 12)), dma((4,)), dma((4,)), dma((4,)), dma((4,)), dma((8,)), dma((8,)),
            dma((4,)), dma((4,)), dma((4,)), dma((4,)),
        ],
        compiler_params=pltpu.CompilerParams(collective_id=0, has_side_effects=True, vmem_limit_bytes=58 << 20),
        cost_estimate=pl.CostEstimate(flops=20_000_000_000, bytes_accessed=20_000_000, transcendentals=0),
    )(
        tap_tokens, project_weight, expand_four, expand_two, shrink_weight, refine_filters, head_matrix,
        head_vector.reshape(1, 128), target,
    )
    pixels = result.reshape(2, 8, 128)[:, :SLOT_DEV].transpose(1, 0, 2).reshape(SLOT_DEV, 32, 8)
    return pixels.transpose(0, 2, 1).reshape(SLOT_DEV, 256)


def solution(mesh):
    in_specs = (
        P("phase", "dp", None), P("phase", None, None), P(), P(), P(), P(None, None, "dp", None), P(), P(), P(),
    )
    return jax.shard_map(
        per_device, mesh=mesh, in_specs=in_specs, out_specs=P(("phase", "dp"), None), check_vma=False
    )
```

time: 712 us -> 88.7 us (0.12); the launches traced: 703 us -> 88.5 us
  waiting for transfers between devices: 465 us -> 0 us
  Pallas kernels: 0 us -> 83.7 us
  blocking collectives: 59 us -> 0 us
  starting transfers between devices: 56.4 us -> 0 us
  local copies, waits for them, and re-layouts: 50 us -> 4.7 us
  matrix products: 37.3 us -> 0 us
  other arithmetic: 20.4 us -> 0.03 us
  between operations: 14.9 us -> 0.03 us
    all_gather x8 -> x0, waiting for transfers between devices: 453 us -> none  [convolve(): whole_matrix = lax.all_gather(matrix, 'dp', axis=0, tiled=True)]
    pallas_call x0 -> x1, Pallas kernels: none -> 83.7 us  [per_device(): pl.pallas_call(kernel, out_shape=jax.ShapeDtypeStruct((16, 128), F32), in...]
    ppermute x24 -> x0, starting transfers between devices: 56.1 us -> none  [the longest x8 31.9 us: padded_2(): lax.ppermute(lax.slice_in_dim(block, block.shape[dim] - width, None, axis...]
    all_gather x1 -> x0, blocking collectives: 48.8 us -> none  [per_device(): portion = lax.all_gather(depth_tiles[None], 'dp', axis=0, tiled=True)]
    dot_general x15 -> x0, matrix products: 37.3 us -> none  [the longest x8 29.1 us: convolve(): result = jnp.dot(patches, whole_matrix, preferred_element_type=jnp.float32)]
    unnamed x67 -> x5, local copies, waits for them, and re-layouts: 31.7 us -> 3.09 us
    unnamed x18 -> x0, other arithmetic: 12.2 us -> none
    ppermute x24 -> x0, waiting for transfers between devices: 11.1 us -> none  [the longest x8 5.96 us: padded_2(): lax.ppermute(lax.slice_in_dim(block, block.shape[dim] - width, None, axis...]
  transfers between devices with their start and end apart: 32 -> 0, of which waited for: 22 -> 0; matrix products, arithmetic and copies ran while one was open for 14% -> 0% of each run, Pallas kernels for 0% -> 0%
where the time goes in v1:
time: 88.7 us; the launch traced here: 88.5 us
  Pallas kernels  83.7 us (94%)
  local copies, waits for them, and re-layouts  4.7 us (5%)
    pallas_call x1, Pallas kernels, per_device(): pl.pallas_call(kernel, out_shape=jax.ShapeDtypeStruct((16, 128), F32), in...  83.7 us
    unnamed x5, local copies, waits for them, and re-layouts  3.09 us

profile of v1, /device:TPU:1, one launch (start us, length us, event | category | flops | bytes accessed | tf_op | source)
XLA Modules:
  0.0 88.5 jit_solution(17164458966827074310)
XLA Ops:
  0.0 0.0 copy-start
  0.0 0.7 copy-done
  0.7 0.1 copy.21
  0.9 0.7 add.34.target_ref
  1.6 1.6 %copy.18.filter_hbm = bf16[4,2,36,256]{3,2,1,0:T(8,128)(2,1)} copy(bf16[4,2,36,256]{3,1,2,0:T(2,128)(2,1)} %param.14) | data formatting | bytes 294912 | tf_op args[5]
  3.2 83.7 %shard_map.91 = f32[16,128]{1,0:T(8,128)} custom-call(bf16[1,512,4096]{2,1,0:T(8,128)(2,1)} %tap_hbm.1, bf16[1,4096,256]{2,1,0:T(8,128)(2,1)} %weight_hbm.1, bf16[256,4096]{1,0:T(8,128)(2,1)} %four_hbm.1, bf16[256,1024]{1,0:T(8,128)(2,1)} %two_hbm.1, bf16[1024,256]{1,0:T(8,128)(2,1)} %shrink_hbm.1, bf16[4,2,36,256]{3,2,1,0:T(8,128)(2,1)} %copy.18.filter_hbm, ...), custom_call_target="tpu_custom_call" | custom-call | flops 20000000000 | bytes 20000000 | tf_op jit(solution)/shard_map/pallas_call | solution.py:447
  86.9 0.7 copy.24
  87.6 0.1 reshape.42
  87.7 0.1 copy.20
  87.8 0.7 reshape.43
  (4 shorter events, 0.0 us)
Async XLA Ops:
  0.0 0.7 copy-start

commit v2 on v1

--- a/solution.py
+++ b/solution.py
@@ -11,6 +11,7 @@
 CH = 256
 SLOT_DEV = 6
 BLOCK = 288
+WHOLE = (0, 1)
 
 OWN = (8, 8, 8, 2)
 HALO = (1, 2, 4, 2)
@@ -28,12 +29,12 @@
 
 
 def kernel(
-    tap_hbm, weight_hbm, four_hbm, two_hbm, shrink_hbm, filter_hbm, head_ref, vector_ref, target_ref,
+    tap_hbm, weight_hbm, four_hbm, two_hbm, shrink_hbm, filter_hbm, head_ref, vector_ref, slot_ref,
     out_ref,
-    filt, own, zbuf, rel, tap, weight, four, two, shrink, proj, gathered, sent,
-    rb0, rb1, rb2, rb3, lift, tok0, tok1, spread,
+    filt, mixed_rows, own, zbuf, rel, tap, weight, four, two, shrink, proj, gathered, sent,
+    rb0, rb1, rb2, rb3, lift, tok0, tok1,
     s0, s1, s2, s3, i0, i1, i2, i3, j0, j1, j2, j3, b0, b1, b2, b3, tiles,
-    own_sem, tap_sem, load_sem, zs, zr, ys, yr, xs, xr, cs, cr, ts, tr, fs, fr, us, ur, vs, vr, ws, wr,
+    own_sem, tap_sem, weight_sem, load_sem, zs, zr, ys, yr, gs, gr, xs, xr, cs, cr, ts, tr, fs, fr, us, ur, vs, vr, ws, wr,
 ):
     x, y, z, c = coords()
     e = x % 2
@@ -41,16 +42,18 @@
     slot = (z % 4) * 2 + c
     received = (rb0, rb1, rb2, rb3)
 
-    own_load = pltpu.make_async_copy(filter_hbm, own, own_sem)
+    own_load = pltpu.make_async_copy(filter_hbm, mixed_rows, own_sem)
     own_load.start()
-    weight_load = pltpu.make_async_copy(weight_hbm.at[0], weight, load_sem.at[0])
-    weight_load.start()
     tap_loads = [
-        pltpu.make_async_copy(tap_hbm.at[0, pl.ds(128 * k, 128)], tap.at[pl.ds(128 * k, 128)], tap_sem.at[k])
+        (
+            pltpu.make_async_copy(weight_hbm.at[0, pl.ds(1024 * k, 1024)], weight.at[pl.ds(1024 * k, 1024)], weight_sem.at[k]),
+            pltpu.make_async_copy(tap_hbm.at[0, :, pl.ds(1024 * k, 1024)], tap.at[k], tap_sem.at[k]),
+        )
         for k in range(4)
     ]
-    for load in tap_loads:
-        load.start()
+    for pair in tap_loads:
+        for load in pair:
+            load.start()
     shrink_load = pltpu.make_async_copy(shrink_hbm, shrink, load_sem.at[1])
     four_load = pltpu.make_async_copy(four_hbm, four, load_sem.at[2])
     two_load = pltpu.make_async_copy(two_hbm, two, load_sem.at[3])
@@ -69,24 +72,27 @@
         pl.semaphore_signal(barrier, inc=1, device_id=did(x, (y + step) % 4, z, c), device_id_type=MESH)
         pl.semaphore_signal(barrier, inc=1, device_id=did((x + step) % 4, y, z, c), device_id_type=MESH)
     own_load.wait()
+    for L in range(4):
+        for m in range(2):
+            own[L, m] = mixed_rows[L, :, m, :]
     pl.semaphore_wait(barrier, 21)
 
-    def zcopy(L, dz):
-        return pltpu.make_async_remote_copy(
-            src_ref=own.at[L, e], dst_ref=zbuf.at[L, slot], send_sem=zs.at[L, dz], recv_sem=zr.at[L, slot],
+    def zcopy(L, o, dz):
+        return pltpu.make_async_remote_copy(
+            src_ref=own.at[L, (e + o) % 2], dst_ref=zbuf.at[L, o, slot], send_sem=zs.at[L, o, dz], recv_sem=zr.at[L, o, slot],
             device_id=did(x, y, (z + dz) % 8, ct), device_id_type=MESH)
 
-    def zsend(L):
+    def zsend(L, o):
         for dz in (4, 3, 5, 2, 6, 1, 7):
-            zcopy(L, dz).start()
+            zcopy(L, o, dz).start()
 
         @pl.when(ct == c)
         def _():
-            pltpu.make_async_copy(own.at[L, e], zbuf.at[L, slot], zr.at[L, slot]).start()
+            pltpu.make_async_copy(own.at[L, (e + o) % 2], zbuf.at[L, o, slot], zr.at[L, o, slot]).start()
 
         @pl.when(ct != c)
         def _():
-            zcopy(L, 0).start()
+            zcopy(L, o, 0).start()
 
     def block(dy, cc, count=BLOCK, start=0):
         return pl.ds(pl.multiple_of((((y + 4 - dy) % 4) * 2 + cc) * BLOCK + start, 16), count)
@@ -109,28 +115,47 @@
             src_ref=ref, dst_ref=ref, send_sem=cs.at[L, k], recv_sem=cr.at[L, k],
             device_id=did(x, y, z, 1 - c), device_id_type=MESH)
 
-    def forward(L, dy):
-        xcopy(L, dy, 0, e).start()
-        xcopy(L, dy, 1, e).start()
-        ccopy(L, dy, e, c, BLOCK, 0, dy).start()
+    def fcopy(L, h, dy):
+        ref = filt.at[2 * L + e, block(dy, c, 144, 144 * h)]
+        return pltpu.make_async_remote_copy(
+            src_ref=ref, dst_ref=ref, send_sem=gs.at[L, h], recv_sem=gr.at[L, h],
+            device_id=did(x, (y + 1 + 2 * h) % 4, z, c), device_id_type=MESH)
+
+    def arrange(L, o):
+        for s in range(8):
+            pltpu.make_async_copy(own.at[L, e], zbuf.at[L, o, s], zr.at[L, o, s]).wait()
+        for s in range(8):
+            rel[pl.ds(36 * s, 36)] = zbuf[L, o, s].astype(F32)
+        filt[2 * L + (e + o) % 2, block(0, c)] = rel[...].astype(BF)
 
     def zy(L):
-        for s in range(8):
-            pltpu.make_async_copy(own.at[L, e], zbuf.at[L, s], zr.at[L, s]).wait()
-        for s in range(8):
-            rel[pl.ds(36 * s, 36)] = zbuf[L, s].astype(F32)
-        filt[2 * L + e, block(0, c)] = rel[...].astype(BF)
-        for dy in (2, 1, 3):
+        arrange(L, 0)
+        for dy in (1, 3):
             ycopy(L, dy, 0).start()
-        forward(L, 0)
-
-    def yx(L):
-        for dy in (1, 3, 2):
-            ycopy(L, dy, dy).wait_recv()
-            forward(L, dy)
-
-    def xc(L):
-        for dy in (0, 1, 3, 2):
+        if L not in WHOLE:
+            for h in range(2):
+                xcopy(L, 0, h, e).start()
+        ccopy(L, 0, e, c, BLOCK, 0, 0).start()
+
+    def za(L):
+        arrange(L, 1)
+        ccopy(L, 0, 1 - e, c, BLOCK, 0, 4).start()
+
+    def yx(L, steps=(1, 3, 2)):
+        for dy in steps:
+            if dy == 2:
+                for h in range(2):
+                    fcopy(L, h, 2).wait_recv()
+                    xcopy(L, 2, h, e).start()
+            else:
+                ycopy(L, dy, dy).wait_recv()
+                fcopy(L, dy // 2, dy).start()
+                for h in range(2):
+                    xcopy(L, dy, h, e).start()
+            ccopy(L, dy, e, c, BLOCK, 0, dy).start()
+
+    def xc(L, steps=(0, 1, 3, 2)):
+        for dy in steps:
             for h in range(2):
                 xcopy(L, dy, h, 1 - e).wait_recv()
                 ccopy(L, dy, 1 - e, c, 144, 144 * h, 4 + dy * 2 + h).start()
@@ -138,34 +163,43 @@
     def fin(L):
         for dy in range(4):
             ccopy(L, dy, e, 1 - c, BLOCK, 0, dy).wait_recv()
-            for h in range(2):
-                ccopy(L, dy, 1 - e, 1 - c, 144, 144 * h, 4 + dy * 2 + h).wait_recv()
+            if dy == 0 and L in WHOLE:
+                ccopy(L, 0, 1 - e, 1 - c, BLOCK, 0, 4).wait_recv()
+            else:
+                for h in range(2):
+                    ccopy(L, dy, 1 - e, 1 - c, 144, 144 * h, 4 + dy * 2 + h).wait_recv()
 
     def sent_filters(L):
-        for dz in range(1, 8):
-            zcopy(L, dz).wait_send()
-
-        @pl.when(ct != c)
-        def _():
-            zcopy(L, 0).wait_send()
-
-        for dy in range(1, 4):
+        for o in range(2 if L in WHOLE else 1):
+            for dz in range(1, 8):
+                zcopy(L, o, dz).wait_send()
+
+            @pl.when(ct != c)
+            def _():
+                zcopy(L, o, 0).wait_send()
+
+        for dy in (1, 3):
             ycopy(L, dy, 0).wait_send()
+            fcopy(L, dy // 2, dy).wait_send()
         for dy in range(4):
             ccopy(L, dy, e, c, BLOCK, 0, dy).wait_send()
-            for h in range(2):
-                xcopy(L, dy, h, e).wait_send()
-                ccopy(L, dy, 1 - e, c, 144, 144 * h, 4 + dy * 2 + h).wait_send()
+            if dy == 0 and L in WHOLE:
+                ccopy(L, 0, 1 - e, c, BLOCK, 0, 4).wait_send()
+            else:
+                for h in range(2):
+                    xcopy(L, dy, h, e).wait_send()
+                    ccopy(L, dy, 1 - e, c, 144, 144 * h, 4 + dy * 2 + h).wait_send()
 
     for L in (3, 2, 1, 0):
-        zsend(L)
-
-    weight_load.wait()
+        zsend(L, 0)
+
     for k in range(4):
-        tap_loads[k].wait()
-        part = jnp.dot(tap[pl.ds(128 * k, 128)], weight[...], preferred_element_type=F32)
+        for load in tap_loads[k]:
+            load.wait()
+        part = jnp.dot(tap[k], weight[pl.ds(1024 * k, 1024)], preferred_element_type=F32)
         for n in range(2):
-            proj[n, pl.ds(128 * k, 128)] = part[:, 128 * n:128 * n + 128]
+            half = part[:, 128 * n:128 * n + 128]
+            proj[n] = half if k == 0 else proj[n] + half
     shrink_load.wait()
 
     @pl.when(x == 3)
@@ -211,11 +245,13 @@
         return pltpu.make_async_remote_copy(
             src_ref=ref, dst_ref=ref, send_sem=fs.at[k], recv_sem=fr.at[k], device_id=did(x, y, z, 1 - c), device_id_type=MESH)
 
+    zy(3)
+    for L in (1, 0):
+        zsend(L, 1)
+    zy(2)
     for k in (3, 2, 1, 0):
         pltpu.make_async_copy(sent.at[pl.ds(0, SENT[k])], window(k, c, x), tr.at[k]).wait()
         halves(k, c).start()
-    zy(3)
-    zy(2)
 
     upper = c == 0
     lift[...] = jnp.zeros_like(lift)
@@ -252,6 +288,8 @@
         return _
 
     lax.fori_loop(0, 16, load_2, 0)
+    yx(3, (1, 3))
+    zy(1)
     halves(1, 1 - c).wait_recv()
 
     def load_1(col, _):
@@ -262,7 +300,9 @@
     halves(0, 1 - c).wait_recv()
 
     def load_0(col, _):
-        tok0[col] = rows_of(0, 1 + col, 16, 1, 32).astype(BF)
+        above = rows_of(0, 1 + col, 16, 1, 32)
+        tok0[0, col] = above.astype(BF)
+        tok0[1, col] = jnp.where(upper, lift[pl.ds(16, 32)], lift[pl.ds(32, 32)]).astype(BF)
         return _
 
     lax.fori_loop(0, 10, load_0, 0)
@@ -271,30 +311,20 @@
     for a in range(2):
         for b in range(2):
             part = jnp.dot(tok1[...].reshape(384, CH), two[:, pl.ds((2 * a + b) * CH, CH)], preferred_element_type=F32)
-            spread[...] = part.astype(BF).astype(F32).reshape(12, 32, CH)
-
-            def place_1(col, _, a=a, b=b):
+            part = part.astype(BF).astype(F32).reshape(12, 32, CH)
+            for col in range(12):
                 for n in range(2):
-                    s1[n, 2 * col + b, pl.ds(a, 20, 2)] = spread[col, pl.ds(0, 20), pl.ds(128 * n, 128)]
-                return _
-
-            lax.fori_loop(0, 12, place_1, 0)
-    yx(3)
-    zy(1)
+                    s1[n, 2 * col + b, pl.ds(a, 20, 2)] = part[col, :20, 128 * n:128 * n + 128]
     four_load.wait()
-    for a in range(4):
+
+    def expand_four(a):
         for b in range(4):
-            part = jnp.dot(tok0[...].reshape(320, CH), four[:, pl.ds((4 * a + b) * CH, CH)], preferred_element_type=F32)
-            spread[pl.ds(0, 10)] = part.astype(BF).astype(F32).reshape(10, 32, CH)
-            first_row, first_col = int(a < 2), int(b < 2)
-
-            def place_0(col, _, a=a, b=b, first_row=first_row, first_col=first_col):
+            part = jnp.dot(
+                tok0[int(a < 2)].reshape(320, CH), four[:, pl.ds((4 * a + b) * CH, CH)], preferred_element_type=F32)
+            part = part.astype(BF).astype(F32).reshape(10, 32, CH)
+            for col in range(9):
                 for n in range(2):
-                    s0[n, 4 * (col + first_col) + b - 2, pl.ds(4 * first_row + a - 2, 17, 4)] = (
-                        spread[col + first_col, pl.ds(first_row, 17), pl.ds(128 * n, 128)])
-                return _
-
-            lax.fori_loop(0, 9, place_0, 0)
+                    s0[n, 4 * col + (b + 2) % 4, pl.ds((a + 2) % 4, 17, 4)] = part[col + int(b < 2), :17, 128 * n:128 * n + 128]
 
     def inside(col, out_halo, own_cols, own_rows, rows):
         row = lax.broadcasted_iota(jnp.int32, (1, rows, 1), 1) + (own_rows * c - out_halo)
@@ -329,6 +359,7 @@
         halo1, cols1, rows1, chunk1, col0, row0 = first
         halo2, cols2, rows2, chunk2, at = second
         build(s, patch, col0, row0, cols1 + 2, rows1)
+        fin(k)
 
         def emit_1(start, result):
             keep = inside((start, chunk1), halo1, own_cols, own_rows, rows1)
@@ -357,25 +388,49 @@
 
         lax.fori_loop(0, cols, step, 0)
 
-    xc(3)
-    yx(2)
+    yx(2, (1, 3))
     zy(0)
-    fin(3)
+    yx(3, (2,))
+    xc(3, (0, 1, 3))
+    expand_four(0)
+    yx(1, (1, 3))
+    xc(3, (2,))
+    yx(2, (2,))
+    xc(2, (0,))
     level(3, s3, i3, j3, b3, 4, 8, (3, 10, 16, 10, 0, 0), (2, 8, 16, 8, 2))
+    xc(2, (1, 3))
+    yx(1, (2,))
     rise(j3, s2, 8, 12)
-    xc(2)
-    yx(1)
-    fin(2)
+    za(1)
+    expand_four(1)
+    yx(0, (1, 3))
+    xc(2, (2,))
+    xc(1, (1, 3))
     level(2, s2, i2, j2, b2, 8, 16, (3, 14, 32, 14, 0, 0), (2, 12, 32, 12, 2))
+    yx(0, (2,))
+    xc(1, (2,))
     rise(j2, s1, 12, 20)
-    xc(1)
-    yx(0)
-    fin(1)
+    za(0)
+    expand_four(2)
+    expand_four(3)
+    xc(0, (1, 3))
     level(1, s1, i1, j1, b1, 16, 32, (2, 20, 48, 10, 1, 1), (1, 18, 48, 9, 3))
+    xc(0, (2,))
     rise(j1, s0, 18, 34)
-    xc(0)
+    build(s0, b0, 0, 0, 36, 80)
     fin(0)
-    level(0, s0, i0, j0, b0, 32, 64, (1, 34, 80, 2, 0, 0), (0, 32, 64, 4, 2))
+
+    def emit_0(start, result):
+        i0[pl.ds(start, 17), pl.ds(0, 80)] = jnp.where(inside((start, 17), 1, 32, 64, 80), result, 0.0)
+
+    conv(b0, 0, 34, 80, 17, emit_0)
+    build(i0, b0, 0, 0, 34, 64)
+
+    def emit_1(start, result):
+        before = jnp.concatenate([s0[n, pl.ds(start + 2, 16), pl.ds(2, 64)] for n in range(2)], axis=-1)
+        j0[pl.ds(start, 16)] = (before + result).astype(BF).astype(F32)
+
+    conv(b0, 1, 32, 64, 16, emit_1)
 
     for t in range(8):
         feature = j0[:, pl.ds(8 * t, 8)].reshape(256, CH).astype(BF)
@@ -383,9 +438,12 @@
         depth = lax.dot_general(
             jnp.broadcast_to(vector_ref[...], (8, 128)), hidden, (((1,), (1,)), ((), ())),
             precision=lax.Precision.HIGHEST, preferred_element_type=F32)
-        for n in range(2):
-            rel[pl.ds(8 * n + t, 1), pl.ds(0, 128)] = depth[0:1, 128 * n:128 * n + 128]
-    tiles[c, y, z] = rel[pl.ds(0, 16), pl.ds(0, 128)].astype(BF)
+        rel[pl.ds(t, 1)] = depth[0:1]
+    origin = lax.broadcasted_iota(jnp.int32, (CH, CH), 0)
+    goal = lax.broadcasted_iota(jnp.int32, (CH, CH), 1)
+    order = jnp.where((origin % 8) * 32 + origin // 8 == goal, 1.0, 0.0).astype(BF)
+    ordered = jnp.dot(rel[pl.ds(0, 8)].astype(BF), order, preferred_element_type=F32)
+    tiles[c, y, z] = jnp.concatenate([ordered[:, :128], ordered[:, 128:]], axis=0).astype(BF)
 
     def ucopy(dz, back):
         ref = tiles.at[c, y, (z + 8 - back) % 8]
@@ -413,9 +471,15 @@
                 tap_copy(k, (k + n) % 4, n).wait_send()
         halves(k, c).wait_send()
     slots = (x * 64 + (y * 8 + z) * 2 + c) * SLOT_DEV
+    tile = lax.broadcasted_iota(jnp.int32, (64, 1024), 1)
+    place = jnp.where((tile % 512) // 16 * 2 + tile // 512 == lax.broadcasted_iota(jnp.int32, (64, 1024), 0), 1.0, 0.0)
+    spots = jnp.dot(slot_ref[x].astype(F32), place, precision=lax.Precision.HIGHEST, preferred_element_type=F32)
+    tile = lax.broadcasted_iota(jnp.int32, (8, 1024), 1)
+    target = jnp.sum(jnp.where(tile % 8 == lax.broadcasted_iota(jnp.int32, (8, 1024), 0), spots, 0.0), axis=0, keepdims=True)
     row = lax.broadcasted_iota(jnp.int32, (16, 1024), 0)
-    wanted = (slots + row % 8) * 2 + row // 8
-    match = jnp.where(target_ref[...] == wanted, 1.0, 0.0).astype(BF)
+    tile = lax.broadcasted_iota(jnp.int32, (16, 1024), 1)
+    wanted = (slots + row % 8).astype(F32)
+    match = jnp.where((target == wanted) & ((tile // 8) % 2 == row // 8), 1.0, 0.0).astype(BF)
     for dz in range(1, 8):
         ucopy(dz, dz).wait_recv()
     for dy in (2, 1, 3):
@@ -426,7 +490,9 @@
         wcopy(dy, c).start()
     for dy in range(4):
         wcopy(dy, 1 - c).wait_recv()
-    out_ref[...] = jnp.dot(match, tiles[...].reshape(1024, 128), preferred_element_type=F32)
+    scene = jnp.dot(match, tiles[...].reshape(1024, 128), preferred_element_type=F32)
+    for n in range(2):
+        out_ref[:, pl.ds(128 * n, 128)] = scene[8 * n:8 * n + SLOT_DEV]
     for dz in range(1, 8):
         ucopy(dz, 0).wait_send()
     for dy in range(1, 4):
@@ -438,40 +504,35 @@
 def per_device(
     tap_tokens, project_weight, expand_four, expand_two, shrink_weight, refine_filters, head_matrix, head_vector, tile_slot
 ):
-    phase = lax.axis_index("phase")
-    mine = lax.dynamic_index_in_dim(tile_slot, phase, 1, keepdims=False).reshape(4, 8, 2, 1, 8).transpose(2, 0, 1, 3, 4)
-    target = (mine * 2 + jnp.arange(2, dtype=jnp.int32).reshape(1, 1, 1, 2, 1)).reshape(1, 1024)
     vmem, dma = pltpu.VMEM, pltpu.SemaphoreType.DMA
     anywhere = pl.BlockSpec(memory_space=pl.ANY)
     inside = pl.BlockSpec(memory_space=pltpu.VMEM)
-    result = pl.pallas_call(
+    return pl.pallas_call(
         kernel,
-        out_shape=jax.ShapeDtypeStruct((16, 128), F32),
+        out_shape=jax.ShapeDtypeStruct((SLOT_DEV, 256), F32),
         in_specs=[anywhere] * 6 + [inside] * 3,
         out_specs=inside,
         scratch_shapes=[
-            vmem((8, 2304, CH), BF), vmem((4, 2, 36, CH), BF), vmem((4, 8, 36, CH), BF), vmem((BLOCK, CH), F32),
-            vmem((512, 4096), BF), vmem((4096, CH), BF), vmem((CH, 4096), BF), vmem((CH, 1024), BF), vmem((1024, CH), BF),
+            vmem((8, 2304, CH), BF), vmem((4, 36, 2, CH), BF), vmem((4, 2, 36, CH), BF), vmem((4, 2, 8, 36, CH), BF), vmem((BLOCK, CH), F32),
+            vmem((4, 512, 1024), BF), vmem((4096, CH), BF), vmem((CH, 4096), BF), vmem((CH, 1024), BF), vmem((1024, CH), BF),
             vmem((2, 512, 128), F32), vmem((128, 1024), F32), vmem((32, 16, CH), BF),
             vmem((2, LEN[0], 16, CH), BF), vmem((2, LEN[1], 16, CH), BF), vmem((2, LEN[2], 16, CH), BF), vmem((2, LEN[3], 16, CH), BF),
-            vmem((64, CH), F32), vmem((10, 32, CH), BF), vmem((12, 32, CH), BF), vmem((12, 32, CH), F32),
+            vmem((64, CH), F32), vmem((2, 10, 32, CH), BF), vmem((12, 32, CH), BF),
             vmem((2, 36, 88, 128), F32), vmem((2, 24, 56, 128), F32), vmem((2, 16, 40, 128), F32), vmem((2, 12, 24, 128), F32),
             vmem((34, 88, CH), F32), vmem((20, 56, CH), F32), vmem((14, 40, CH), F32), vmem((10, 24, CH), F32),
             vmem((32, 64, CH), F32), vmem((18, 48, CH), F32), vmem((12, 32, CH), F32), vmem((8, 16, CH), F32),
             vmem((3, 36, 80, CH), BF), vmem((3, 22, 48, CH), BF), vmem((3, 16, 32, CH), BF), vmem((3, 12, 16, CH), BF),
             vmem((2, 4, 8, 16, 128), BF),
-            dma, dma((4,)), dma((4,)), dma((4, 8)), dma((4, 8)), dma((4, 4)), dma((4, 4)), dma((4, 4, 2)), dma((4, 4, 2)),
+            dma, dma((4,)), dma((4,)), dma((4,)), dma((4, 2, 8)), dma((4, 2, 8)), dma((4, 4)), dma((4, 4)), dma((4, 2)), dma((4, 2)), dma((4, 4, 2)), dma((4, 4, 2)),
             dma((4, 12)), dma((4, 12)), dma((4,)), dma((4,)), dma((4,)), dma((4,)), dma((8,)), dma((8,)),
             dma((4,)), dma((4,)), dma((4,)), dma((4,)),
         ],
         compiler_params=pltpu.CompilerParams(collective_id=0, has_side_effects=True, vmem_limit_bytes=58 << 20),
         cost_estimate=pl.CostEstimate(flops=20_000_000_000, bytes_accessed=20_000_000, transcendentals=0),
     )(
-        tap_tokens, project_weight, expand_four, expand_two, shrink_weight, refine_filters, head_matrix,
-        head_vector.reshape(1, 128), target,
+        tap_tokens, project_weight, expand_four, expand_two, shrink_weight, refine_filters.transpose(0, 2, 1, 3), head_matrix,
+        head_vector.reshape(1, 128), tile_slot.transpose(1, 2, 0),
     )
-    pixels = result.reshape(2, 8, 128)[:, :SLOT_DEV].transpose(1, 0, 2).reshape(SLOT_DEV, 32, 8)
-    return pixels.transpose(0, 2, 1).reshape(SLOT_DEV, 256)
 
 
 def solution(mesh):

time: 88.7 us -> 74.1 us (0.84)
  Pallas kernels: 83.7 us -> 72.6 us
  local copies, waits for them, and re-layouts: 4.7 us -> 1.3 us
    pallas_call x1, Pallas kernels: 83.7 us -> 72.6 us  [per_device(): pl.pallas_call(kernel, out_shape=jax.ShapeDtypeStruct((SLOT_DEV, 256), F3...]
    unnamed x5 -> x1, local copies, waits for them, and re-layouts: 3.09 us -> 1.3 us
where the time goes in v2:
time: 74.1 us; the launch traced here: 73.9 us
  Pallas kernels  72.6 us (98%)
  local copies, waits for them, and re-layouts  1.3 us (2%)
    pallas_call x1, Pallas kernels, per_device(): pl.pallas_call(kernel, out_shape=jax.ShapeDtypeStruct((SLOT_DEV, 256), F3...  72.6 us

profile of v2, /device:TPU:1, one launch (start us, length us, event | category | flops | bytes accessed | tf_op | source)
XLA Modules:
  0.0 73.9 jit_solution(4562756573362929486)
XLA Ops:
  0.0 72.6 %shard_map.91 = f32[6,256]{1,0:T(8,128)} custom-call(bf16[1,512,4096]{2,1,0:T(8,128)(2,1)} %tap_hbm.1, bf16[1,4096,256]{2,1,0:T(8,128)(2,1)} %weight_hbm.1, bf16[256,4096]{1,0:T(8,128)(2,1)} %four_hbm.1, bf16[256,1024]{1,0:T(8,128)(2,1)} %two_hbm.1, bf16[1024,256]{1,0:T(8,128)(2,1)} %shrink_hbm.1, bf16[4,36,2,256]{3,2,1,0:T(2,128)(2,1)} %bitcast.3, ...), custom_call_target="tpu_custom_call" | custom-call | flops 20000000000 | bytes 20000000 | tf_op jit(solution)/shard_map/pallas_call | solution.py:510
  72.6 1.3 %copy.11 = f32[6,256]{1,0:T(8,128)} copy(f32[6,256]{1,0:T(8,128)} %shard_map.91) | data formatting | bytes 12288

commit v3 on v2

--- a/solution.py
+++ b/solution.py
@@ -31,10 +31,10 @@
 def kernel(
     tap_hbm, weight_hbm, four_hbm, two_hbm, shrink_hbm, filter_hbm, head_ref, vector_ref, slot_ref,
     out_ref,
-    filt, mixed_rows, own, zbuf, rel, tap, weight, four, two, shrink, proj, gathered, sent,
+    filt, mixed_rows, own, zone, ztwo, rel, tap, weight, four, two, shrink, proj, gathered, sent,
     rb0, rb1, rb2, rb3, lift, tok0, tok1,
-    s0, s1, s2, s3, i0, i1, i2, i3, j0, j1, j2, j3, b0, b1, b2, b3, tiles,
-    own_sem, tap_sem, weight_sem, load_sem, zs, zr, ys, yr, gs, gr, xs, xr, cs, cr, ts, tr, fs, fr, us, ur, vs, vr, ws, wr,
+    s0, s1, s2, s3, i0, i1, i2, i3, j0, j1, j2, j3, b0, b1, b2, b3, mine, tiles,
+    own_sem, tap_sem, weight_sem, load_sem, zs, zr, ys, yr, gs, gr, xs, xr, cs, cr, ts, tr, fs, fr, us, ur, ws, wr,
 ):
     x, y, z, c = coords()
     e = x % 2
@@ -71,127 +71,110 @@
     for step in range(1, 4):
         pl.semaphore_signal(barrier, inc=1, device_id=did(x, (y + step) % 4, z, c), device_id_type=MESH)
         pl.semaphore_signal(barrier, inc=1, device_id=did((x + step) % 4, y, z, c), device_id_type=MESH)
+    for dy in range(1, 4):
+        for dz in range(1, 8):
+            pl.semaphore_signal(barrier, inc=1, device_id=did(x, (y + dy) % 4, (z + dz) % 8, c), device_id_type=MESH)
     own_load.wait()
     for L in range(4):
         for m in range(2):
-            own[L, m] = mixed_rows[L, :, m, :]
-    pl.semaphore_wait(barrier, 21)
-
-    def zcopy(L, o, dz):
+            own[m, L] = mixed_rows[L, :, m, :]
+    pl.semaphore_wait(barrier, 42)
+
+    def zends(q):
+        if q < 2:
+            return own.at[e, pl.ds(3 - q, 1)], zone.at[q, slot]
+        return own.at[(e + q) % 2, pl.ds(0, 2)], ztwo.at[q - 2, slot]
+
+    def zcopy(q, dz):
+        source, target = zends(q)
         return pltpu.make_async_remote_copy(
-            src_ref=own.at[L, (e + o) % 2], dst_ref=zbuf.at[L, o, slot], send_sem=zs.at[L, o, dz], recv_sem=zr.at[L, o, slot],
+            src_ref=source, dst_ref=target, send_sem=zs.at[q], recv_sem=zr.at[q],
             device_id=did(x, y, (z + dz) % 8, ct), device_id_type=MESH)
 
-    def zsend(L, o):
+    def zsend(q):
         for dz in (4, 3, 5, 2, 6, 1, 7):
-            zcopy(L, o, dz).start()
+            zcopy(q, dz).start()
 
         @pl.when(ct == c)
         def _():
-            pltpu.make_async_copy(own.at[L, (e + o) % 2], zbuf.at[L, o, slot], zr.at[L, o, slot]).start()
+            source, target = zends(q)
+            pltpu.make_async_copy(source, target, zr.at[q]).start()
 
         @pl.when(ct != c)
         def _():
-            zcopy(L, o, 0).start()
+            zcopy(q, 0).start()
+
+    def zwait(q, sem, count):
+        ref = (zone.at[q] if q < 2 else ztwo.at[q - 2]).at[pl.ds(0, count)]
+        pltpu.make_async_copy(ref, ref, sem).wait()
+
+    def wait_rows(sem, count):
+        ref = filt.at[0, pl.ds(0, count)]
+        pltpu.make_async_copy(ref, ref, sem).wait()
 
     def block(dy, cc, count=BLOCK, start=0):
         return pl.ds(pl.multiple_of((((y + 4 - dy) % 4) * 2 + cc) * BLOCK + start, 16), count)
 
-    def ycopy(L, dy, back):
-        ref = filt.at[2 * L + e, block(back, c)]
-        return pltpu.make_async_remote_copy(
-            src_ref=ref, dst_ref=ref, send_sem=ys.at[L, dy], recv_sem=yr.at[L, dy],
-            device_id=did(x, (y + dy) % 4, z, c), device_id_type=MESH)
-
-    def xcopy(L, dy, h, f):
-        ref = filt.at[2 * L + f, block(dy, c, 144, 144 * h)]
-        return pltpu.make_async_remote_copy(
-            src_ref=ref, dst_ref=ref, send_sem=xs.at[L, dy, h], recv_sem=xr.at[L, dy, h],
-            device_id=did((x + 1 + 2 * h) % 4, y, z, c), device_id_type=MESH)
-
-    def ccopy(L, dy, f, cc, count, start, k):
-        ref = filt.at[2 * L + f, block(dy, cc, count, start)]
-        return pltpu.make_async_remote_copy(
-            src_ref=ref, dst_ref=ref, send_sem=cs.at[L, k], recv_sem=cr.at[L, k],
-            device_id=did(x, y, z, 1 - c), device_id_type=MESH)
-
-    def fcopy(L, h, dy):
-        ref = filt.at[2 * L + e, block(dy, c, 144, 144 * h)]
-        return pltpu.make_async_remote_copy(
-            src_ref=ref, dst_ref=ref, send_sem=gs.at[L, h], recv_sem=gr.at[L, h],
-            device_id=did(x, (y + 1 + 2 * h) % 4, z, c), device_id_type=MESH)
+    def send(ref, send_sem, recv_sem, device):
+        pltpu.make_async_remote_copy(
+            src_ref=ref, dst_ref=ref, send_sem=send_sem, recv_sem=recv_sem, device_id=device, device_id_type=MESH).start()
+
+    def xsend(L, dy):
+        for h in range(2):
+            send(filt.at[2 * L + e, block(dy, c, 144, 144 * h)], xs.at[L], xr.at[L, dy], did((x + 1 + 2 * h) % 4, y, z, c))
+
+    def csend(L, dy, f):
+        send(filt.at[2 * L + f, block(dy, c)], cs.at[L], cr.at[L], did(x, y, z, 1 - c))
 
     def arrange(L, o):
         for s in range(8):
-            pltpu.make_async_copy(own.at[L, e], zbuf.at[L, o, s], zr.at[L, o, s]).wait()
-        for s in range(8):
-            rel[pl.ds(36 * s, 36)] = zbuf[L, o, s].astype(F32)
+            rows = zone[3 - L, s, 0] if L > 1 else ztwo[o, s, L]
+            rel[pl.ds(36 * s, 36)] = rows.astype(F32)
         filt[2 * L + (e + o) % 2, block(0, c)] = rel[...].astype(BF)
 
     def zy(L):
+        if L:
+            zwait(min(3 - L, 2), zr.at[min(3 - L, 2)], 8)
         arrange(L, 0)
         for dy in (1, 3):
-            ycopy(L, dy, 0).start()
+            send(filt.at[2 * L + e, block(0, c)], ys.at[L], yr.at[L, dy], did(x, (y + dy) % 4, z, c))
         if L not in WHOLE:
-            for h in range(2):
-                xcopy(L, 0, h, e).start()
-        ccopy(L, 0, e, c, BLOCK, 0, 0).start()
+            xsend(L, 0)
+        csend(L, 0, e)
 
     def za(L):
+        if L:
+            zwait(3, zr.at[3], 8)
         arrange(L, 1)
-        ccopy(L, 0, 1 - e, c, BLOCK, 0, 4).start()
+        csend(L, 0, 1 - e)
 
     def yx(L, steps=(1, 3, 2)):
         for dy in steps:
             if dy == 2:
-                for h in range(2):
-                    fcopy(L, h, 2).wait_recv()
-                    xcopy(L, 2, h, e).start()
+                wait_rows(gr.at[L], BLOCK)
             else:
-                ycopy(L, dy, dy).wait_recv()
-                fcopy(L, dy // 2, dy).start()
-                for h in range(2):
-                    xcopy(L, dy, h, e).start()
-            ccopy(L, dy, e, c, BLOCK, 0, dy).start()
+                wait_rows(yr.at[L, dy], BLOCK)
+                h = dy // 2
+                send(filt.at[2 * L + e, block(dy, c, 144, 144 * h)], gs.at[L], gr.at[L], did(x, (y + 1 + 2 * h) % 4, z, c))
+            xsend(L, dy)
+            csend(L, dy, e)
 
     def xc(L, steps=(0, 1, 3, 2)):
         for dy in steps:
-            for h in range(2):
-                xcopy(L, dy, h, 1 - e).wait_recv()
-                ccopy(L, dy, 1 - e, c, 144, 144 * h, 4 + dy * 2 + h).start()
+            wait_rows(xr.at[L, dy], BLOCK)
+            csend(L, dy, 1 - e)
 
     def fin(L):
-        for dy in range(4):
-            ccopy(L, dy, e, 1 - c, BLOCK, 0, dy).wait_recv()
-            if dy == 0 and L in WHOLE:
-                ccopy(L, 0, 1 - e, 1 - c, BLOCK, 0, 4).wait_recv()
-            else:
-                for h in range(2):
-                    ccopy(L, dy, 1 - e, 1 - c, 144, 144 * h, 4 + dy * 2 + h).wait_recv()
+        wait_rows(cr.at[L], 2304)
 
     def sent_filters(L):
-        for o in range(2 if L in WHOLE else 1):
-            for dz in range(1, 8):
-                zcopy(L, o, dz).wait_send()
-
-            @pl.when(ct != c)
-            def _():
-                zcopy(L, o, 0).wait_send()
-
-        for dy in (1, 3):
-            ycopy(L, dy, 0).wait_send()
-            fcopy(L, dy // 2, dy).wait_send()
-        for dy in range(4):
-            ccopy(L, dy, e, c, BLOCK, 0, dy).wait_send()
-            if dy == 0 and L in WHOLE:
-                ccopy(L, 0, 1 - e, c, BLOCK, 0, 4).wait_send()
-            else:
-                for h in range(2):
-                    xcopy(L, dy, h, e).wait_send()
-                    ccopy(L, dy, 1 - e, c, 144, 144 * h, 4 + dy * 2 + h).wait_send()
-
-    for L in (3, 2, 1, 0):
-        zsend(L, 0)
+        wait_rows(ys.at[L], 2 * BLOCK)
+        wait_rows(gs.at[L], BLOCK)
+        wait_rows(xs.at[L], (3 if L in WHOLE else 4) * BLOCK)
+        wait_rows(cs.at[L], 2304)
+
+    for q in range(3):
+        zsend(q)
 
     for k in range(4):
         for load in tap_loads[k]:
@@ -246,8 +229,7 @@
             src_ref=ref, dst_ref=ref, send_sem=fs.at[k], recv_sem=fr.at[k], device_id=did(x, y, z, 1 - c), device_id_type=MESH)
 
     zy(3)
-    for L in (1, 0):
-        zsend(L, 1)
+    zsend(3)
     zy(2)
     for k in (3, 2, 1, 0):
         pltpu.make_async_copy(sent.at[pl.ds(0, SENT[k])], window(k, c, x), tr.at[k]).wait()
@@ -410,11 +392,11 @@
     yx(0, (2,))
     xc(1, (2,))
     rise(j2, s1, 12, 20)
+    level(1, s1, i1, j1, b1, 16, 32, (2, 20, 48, 10, 1, 1), (1, 18, 48, 9, 3))
     za(0)
+    xc(0, (1, 3))
     expand_four(2)
     expand_four(3)
-    xc(0, (1, 3))
-    level(1, s1, i1, j1, b1, 16, 32, (2, 20, 48, 10, 1, 1), (1, 18, 48, 9, 3))
     xc(0, (2,))
     rise(j1, s0, 18, 34)
     build(s0, b0, 0, 0, 36, 80)
@@ -443,27 +425,30 @@
     goal = lax.broadcasted_iota(jnp.int32, (CH, CH), 1)
     order = jnp.where((origin % 8) * 32 + origin // 8 == goal, 1.0, 0.0).astype(BF)
     ordered = jnp.dot(rel[pl.ds(0, 8)].astype(BF), order, preferred_element_type=F32)
-    tiles[c, y, z] = jnp.concatenate([ordered[:, :128], ordered[:, 128:]], axis=0).astype(BF)
-
-    def ucopy(dz, back):
-        ref = tiles.at[c, y, (z + 8 - back) % 8]
-        return pltpu.make_async_remote_copy(
-            src_ref=ref, dst_ref=ref, send_sem=us.at[dz], recv_sem=ur.at[dz], device_id=did(x, y, (z + dz) % 8, c), device_id_type=MESH)
-
-    def vcopy(dy, back):
-        ref = tiles.at[c, (y + 4 - back) % 4]
-        return pltpu.make_async_remote_copy(
-            src_ref=ref, dst_ref=ref, send_sem=vs.at[dy], recv_sem=vr.at[dy], device_id=did(x, (y + dy) % 4, z, c), device_id_type=MESH)
-
-    def wcopy(dy, cc):
-        ref = tiles.at[cc, (y + 4 - dy) % 4]
-        return pltpu.make_async_remote_copy(
-            src_ref=ref, dst_ref=ref, send_sem=ws.at[dy], recv_sem=wr.at[dy], device_id=did(x, y, z, 1 - c), device_id_type=MESH)
-
-    for dz in (4, 3, 5, 2, 6, 1, 7):
-        ucopy(dz, 0).start()
+    mine[...] = jnp.concatenate([ordered[:, :128], ordered[:, 128:]], axis=0).astype(BF)
+
+    for dz in (4, 3, 5, 2, 6, 1, 7, 0):
+        for dy in (2, 1, 3, 0):
+            if dy or dz:
+                send_to = did(x, (y + dy) % 4, (z + dz) % 8, c)
+                pltpu.make_async_remote_copy(
+                    src_ref=mine, dst_ref=tiles.at[c, y, z], send_sem=us.at[int(dy == 0)], recv_sem=ur.at[0],
+                    device_id=send_to, device_id_type=MESH).start()
+    pltpu.make_async_copy(mine, tiles.at[c, y, z], ur.at[0]).start()
+
     for L in (3, 2, 1, 0):
         sent_filters(L)
+
+    @pl.when(ct == c)
+    def _():
+        for q in range(4):
+            zwait(q, zs.at[q], 7)
+
+    @pl.when(ct != c)
+    def _():
+        for q in range(4):
+            zwait(q, zs.at[q], 8)
+
     for k in range(4):
         @pl.when(x == k)
         def _():
@@ -480,25 +465,17 @@
     tile = lax.broadcasted_iota(jnp.int32, (16, 1024), 1)
     wanted = (slots + row % 8).astype(F32)
     match = jnp.where((target == wanted) & ((tile // 8) % 2 == row // 8), 1.0, 0.0).astype(BF)
-    for dz in range(1, 8):
-        ucopy(dz, dz).wait_recv()
-    for dy in (2, 1, 3):
-        vcopy(dy, 0).start()
-    wcopy(0, c).start()
-    for dy in (1, 3, 2):
-        vcopy(dy, dy).wait_recv()
-        wcopy(dy, c).start()
-    for dy in range(4):
-        wcopy(dy, 1 - c).wait_recv()
+    pltpu.make_async_copy(tiles.at[c], tiles.at[c], ur.at[0]).wait()
+    to_other = pltpu.make_async_remote_copy(
+        src_ref=tiles.at[c], dst_ref=tiles.at[c], send_sem=ws.at[0], recv_sem=wr.at[0], device_id=did(x, y, z, 1 - c), device_id_type=MESH)
+    to_other.start()
+    pltpu.make_async_copy(tiles.at[1 - c], tiles.at[1 - c], wr.at[0]).wait()
     scene = jnp.dot(match, tiles[...].reshape(1024, 128), preferred_element_type=F32)
     for n in range(2):
         out_ref[:, pl.ds(128 * n, 128)] = scene[8 * n:8 * n + SLOT_DEV]
-    for dz in range(1, 8):
-        ucopy(dz, 0).wait_send()
-    for dy in range(1, 4):
-        vcopy(dy, 0).wait_send()
-    for dy in range(4):
-        wcopy(dy, c).wait_send()
+    pltpu.make_async_copy(tiles.at[c, pl.ds(0, 3)], tiles.at[c, pl.ds(0, 3)], us.at[0]).wait()
+    pltpu.make_async_copy(tiles.at[c, 0, pl.ds(0, 7)], tiles.at[c, 0, pl.ds(0, 7)], us.at[1]).wait()
+    to_other.wait_send()
 
 
 def per_device(
@@ -513,7 +490,7 @@
         in_specs=[anywhere] * 6 + [inside] * 3,
         out_specs=inside,
         scratch_shapes=[
-            vmem((8, 2304, CH), BF), vmem((4, 36, 2, CH), BF), vmem((4, 2, 36, CH), BF), vmem((4, 2, 8, 36, CH), BF), vmem((BLOCK, CH), F32),
+            vmem((8, 2304, CH), BF), vmem((4, 36, 2, CH), BF), vmem((2, 4, 36, CH), BF), vmem((2, 8, 1, 36, CH), BF), vmem((2, 8, 2, 36, CH), BF), vmem((BLOCK, CH), F32),
             vmem((4, 512, 1024), BF), vmem((4096, CH), BF), vmem((CH, 4096), BF), vmem((CH, 1024), BF), vmem((1024, CH), BF),
             vmem((2, 512, 128), F32), vmem((128, 1024), F32), vmem((32, 16, CH), BF),
             vmem((2, LEN[0], 16, CH), BF), vmem((2, LEN[1], 16, CH), BF), vmem((2, LEN[2], 16, CH), BF), vmem((2, LEN[3], 16, CH), BF),
@@ -522,10 +499,10 @@
             vmem((34, 88, CH), F32), vmem((20, 56, CH), F32), vmem((14, 40, CH), F32), vmem((10, 24, CH), F32),
             vmem((32, 64, CH), F32), vmem((18, 48, CH), F32), vmem((12, 32, CH), F32), vmem((8, 16, CH), F32),
             vmem((3, 36, 80, CH), BF), vmem((3, 22, 48, CH), BF), vmem((3, 16, 32, CH), BF), vmem((3, 12, 16, CH), BF),
-            vmem((2, 4, 8, 16, 128), BF),
-            dma, dma((4,)), dma((4,)), dma((4,)), dma((4, 2, 8)), dma((4, 2, 8)), dma((4, 4)), dma((4, 4)), dma((4, 2)), dma((4, 2)), dma((4, 4, 2)), dma((4, 4, 2)),
-            dma((4, 12)), dma((4, 12)), dma((4,)), dma((4,)), dma((4,)), dma((4,)), dma((8,)), dma((8,)),
-            dma((4,)), dma((4,)), dma((4,)), dma((4,)),
+            vmem((16, 128), BF), vmem((2, 4, 8, 16, 128), BF),
+            dma, dma((4,)), dma((4,)), dma((4,)), dma((4,)), dma((4,)), dma((4,)), dma((4, 4)), dma((4,)), dma((4,)),
+            dma((4,)), dma((4, 4)), dma((4,)), dma((4,)), dma((4,)), dma((4,)), dma((4,)), dma((4,)), dma((8,)), dma((8,)),
+            dma((4,)), dma((4,)),
         ],
         compiler_params=pltpu.CompilerParams(collective_id=0, has_side_effects=True, vmem_limit_bytes=58 << 20),
         cost_estimate=pl.CostEstimate(flops=20_000_000_000, bytes_accessed=20_000_000, transcendentals=0),

time: 74.1 us -> 73.1 us (0.987)
  Pallas kernels: 72.6 us -> 71.6 us
    pallas_call x1, Pallas kernels: 72.6 us -> 71.6 us  [per_device(): pl.pallas_call(kernel, out_shape=jax.ShapeDtypeStruct((SLOT_DEV, 256), F3...]
where the time goes in v3:
time: 73.1 us; the launch traced here: 72.9 us
  Pallas kernels  71.6 us (98%)
  local copies, waits for them, and re-layouts  1.3 us (2%)
    pallas_call x1, Pallas kernels, per_device(): pl.pallas_call(kernel, out_shape=jax.ShapeDtypeStruct((SLOT_DEV, 256), F3...  71.6 us

profile of v3, /device:TPU:1, one launch (start us, length us, event | category | flops | bytes accessed | tf_op | source)
XLA Modules:
  0.0 72.9 jit_solution(10309371932120452069)
XLA Ops:
  0.0 71.6 %shard_map.91 = f32[6,256]{1,0:T(8,128)} custom-call(bf16[1,512,4096]{2,1,0:T(8,128)(2,1)} %tap_hbm.1, bf16[1,4096,256]{2,1,0:T(8,128)(2,1)} %weight_hbm.1, bf16[256,4096]{1,0:T(8,128)(2,1)} %four_hbm.1, bf16[256,1024]{1,0:T(8,128)(2,1)} %two_hbm.1, bf16[1024,256]{1,0:T(8,128)(2,1)} %shrink_hbm.1, bf16[4,36,2,256]{3,2,1,0:T(2,128)(2,1)} %bitcast.3, ...), custom_call_target="tpu_custom_call" | custom-call | flops 20000000000 | bytes 20000000 | tf_op jit(solution)/shard_map/pallas_call | solution.py:487
  71.6 1.3 %copy.11 = f32[6,256]{1,0:T(8,128)} copy(f32[6,256]{1,0:T(8,128)} %shard_map.91) | data formatting | bytes 12288

commit v4 on v3

--- a/solution.py
+++ b/solution.py
@@ -33,7 +33,7 @@
     out_ref,
     filt, mixed_rows, own, zone, ztwo, rel, tap, weight, four, two, shrink, proj, gathered, sent,
     rb0, rb1, rb2, rb3, lift, tok0, tok1,
-    s0, s1, s2, s3, i0, i1, i2, i3, j0, j1, j2, j3, b0, b1, b2, b3, mine, tiles,
+    s0, s1, s2, s3, i0, i1, i2, i3, j0, j1, j2, j3, b0, b1, b2, b3, column, mine, tiles,
     own_sem, tap_sem, weight_sem, load_sem, zs, zr, ys, yr, gs, gr, xs, xr, cs, cr, ts, tr, fs, fr, us, ur, ws, wr,
 ):
     x, y, z, c = coords()
@@ -235,6 +235,7 @@
         pltpu.make_async_copy(sent.at[pl.ds(0, SENT[k])], window(k, c, x), tr.at[k]).wait()
         halves(k, c).start()
 
+    column[...] = jnp.broadcast_to(vector_ref[...], (128, 128)).T
     upper = c == 0
     lift[...] = jnp.zeros_like(lift)
 
@@ -414,18 +415,21 @@
 
     conv(b0, 1, 32, 64, 16, emit_1)
 
-    for t in range(8):
-        feature = j0[:, pl.ds(8 * t, 8)].reshape(256, CH).astype(BF)
+    pixel = lax.broadcasted_iota(jnp.int32, (256, 128), 0)
+    goal = (pixel % 8) * 32 + pixel // 8 - lax.broadcasted_iota(jnp.int32, (256, 128), 1)
+
+    tile_row = lax.broadcasted_iota(jnp.int32, (16, 128), 0)
+
+    def head(t, done):
+        feature = j0[:, pl.ds(pl.multiple_of(8 * t, 8), 8)].reshape(256, CH).astype(BF)
         hidden = jnp.maximum(jnp.dot(feature, head_ref[...], preferred_element_type=F32), 0.0)
-        depth = lax.dot_general(
-            jnp.broadcast_to(vector_ref[...], (8, 128)), hidden, (((1,), (1,)), ((), ())),
-            precision=lax.Precision.HIGHEST, preferred_element_type=F32)
-        rel[pl.ds(t, 1)] = depth[0:1]
-    origin = lax.broadcasted_iota(jnp.int32, (CH, CH), 0)
-    goal = lax.broadcasted_iota(jnp.int32, (CH, CH), 1)
-    order = jnp.where((origin % 8) * 32 + origin // 8 == goal, 1.0, 0.0).astype(BF)
-    ordered = jnp.dot(rel[pl.ds(0, 8)].astype(BF), order, preferred_element_type=F32)
-    mine[...] = jnp.concatenate([ordered[:, :128], ordered[:, 128:]], axis=0).astype(BF)
+        depth = jnp.dot(hidden, column[...], precision=lax.Precision.HIGHEST, preferred_element_type=F32)
+        for n in range(2):
+            line = jnp.sum(jnp.where(goal == 128 * n, depth, 0.0), axis=0, keepdims=True)
+            done = jnp.where(tile_row == 8 * n + t, line, done)
+        return done
+
+    mine[...] = lax.fori_loop(0, 8, head, jnp.zeros((16, 128), F32), unroll=8).astype(BF)
 
     for dz in (4, 3, 5, 2, 6, 1, 7, 0):
         for dy in (2, 1, 3, 0):
@@ -499,7 +503,7 @@
             vmem((34, 88, CH), F32), vmem((20, 56, CH), F32), vmem((14, 40, CH), F32), vmem((10, 24, CH), F32),
             vmem((32, 64, CH), F32), vmem((18, 48, CH), F32), vmem((12, 32, CH), F32), vmem((8, 16, CH), F32),
             vmem((3, 36, 80, CH), BF), vmem((3, 22, 48, CH), BF), vmem((3, 16, 32, CH), BF), vmem((3, 12, 16, CH), BF),
-            vmem((16, 128), BF), vmem((2, 4, 8, 16, 128), BF),
+            vmem((128, 128), F32), vmem((16, 128), BF), vmem((2, 4, 8, 16, 128), BF),
             dma, dma((4,)), dma((4,)), dma((4,)), dma((4,)), dma((4,)), dma((4,)), dma((4, 4)), dma((4,)), dma((4,)),
             dma((4,)), dma((4, 4)), dma((4,)), dma((4,)), dma((4,)), dma((4,)), dma((4,)), dma((4,)), dma((8,)), dma((8,)),
             dma((4,)), dma((4,)),

time: 73.1 us -> 73 us (level)
  no operation moved by 1% of the time
where the time goes in v4:
time: 73 us; the launch traced here: 72.8 us
  Pallas kernels  71.5 us (98%)
  local copies, waits for them, and re-layouts  1.3 us (2%)
    pallas_call x1, Pallas kernels, per_device(): pl.pallas_call(kernel, out_shape=jax.ShapeDtypeStruct((SLOT_DEV, 256), F3...  71.5 us

profile of v4, /device:TPU:1, one launch (start us, length us, event | category | flops | bytes accessed | tf_op | source)
XLA Modules:
  0.0 72.8 jit_solution(10168539227442080114)
XLA Ops:
  0.0 71.5 %shard_map.91 = f32[6,256]{1,0:T(8,128)} custom-call(bf16[1,512,4096]{2,1,0:T(8,128)(2,1)} %tap_hbm.1, bf16[1,4096,256]{2,1,0:T(8,128)(2,1)} %weight_hbm.1, bf16[256,4096]{1,0:T(8,128)(2,1)} %four_hbm.1, bf16[256,1024]{1,0:T(8,128)(2,1)} %two_hbm.1, bf16[1024,256]{1,0:T(8,128)(2,1)} %shrink_hbm.1, bf16[4,36,2,256]{3,2,1,0:T(2,128)(2,1)} %bitcast.3, ...), custom_call_target="tpu_custom_call" | custom-call | flops 20000000000 | bytes 20000000 | tf_op jit(solution)/shard_map/pallas_call | solution.py:491
  71.5 1.3 %copy.11 = f32[6,256]{1,0:T(8,128)} copy(f32[6,256]{1,0:T(8,128)} %shard_map.91) | data formatting | bytes 12288
